TPU v7x, 32 devices: a whole 2x2x4 slice. The times are simulated.
32 devices in a mesh: grp: 2 (over x), lon: 16 (over z, y, core).
Axes of the slice: x: 2, y: 2, z: 4, core: 2. Of those that a mesh axis runs over, the one named last changes fastest.
Arguments:
- tracers: float32 [10, 4, 256, 2880], P('grp', None, 'lon'), parts along dimension 0, may hold values from -6 to 6
- east_courant: float32 [8, 256, 2880], P('grp', 'lon'), parts along dimension 0, may hold values from -0.3 to 0.3
- north_courant: float32 [8, 256, 2880], P('grp', 'lon'), parts along dimension 0, may hold values from -0.3 to 0.3
- spectrum: float32 [64, 2880], replicated, may hold values from 0.05 to 1
- filter_index: int32 [256], replicated, may hold values from 0 to 63
Outputs:
- updated: float32 [10, 4, 256, 2880], P('grp', None, 'lon'), parts along dimension 0
There are 2 independent parts, one for each index of `grp`. A program takes and returns all parts, laid end to end along the dimension named above; an argument that names none is the same for every part. Nothing has to cross between parts.
All inputs are finite; a program needn't handle non-finite values.
Results may differ from a plain program's by a relative error of at most 0.00075.
Values may be sent and summed in bfloat16 or wider, within the bound.
A program may use at most 128 MiB of HBM per device.

v0:
```python
import math

import jax
import jax.numpy as jnp
from jax import lax
from jax.sharding import PartitionSpec as P


def extended(block, sides, width):
    for axis, dim in sides:
        count = lax.axis_size(axis)
        forward = [(i, i + 1) for i in range(count - 1)]
        backward = [(target, source) for source, target in forward]
        low = lax.ppermute(
            lax.slice_in_dim(block, block.shape[dim] - width, None, axis=dim), axis, forward
        )
        high = lax.ppermute(lax.slice_in_dim(block, 0, width, axis=dim), axis, backward)
        block = jnp.concatenate([low, block, high], axis=dim)
    return block


def from_behind(x, axis, by):
    count = lax.axis_size(axis)
    pairs = [(i, i + by) for i in range(count) if 0 <= i + by < count]
    return lax.ppermute(x, axis, pairs)


def min_mod(left, right):
    return jnp.maximum(jnp.minimum(left, right), 0.0) + jnp.minimum(jnp.maximum(left, right), 0.0)


def face_flux(left_q, left_s, right_q, right_s, courant):
    return jnp.maximum(courant, 0.0) * (left_q + 0.5 * (1.0 - courant) * left_s) + jnp.minimum(
        courant, 0.0
    ) * (right_q - 0.5 * (1.0 + courant) * right_s)


def tendency(padded, south_courant, north_courant, east_courant, global_rows, total_rows):
    center = padded[:, :, 2:-2]
    slopes = min_mod(padded[:, :, 2:] - padded[:, :, 1:-1], padded[:, :, 1:-1] - padded[:, :, :-2])
    north = face_flux(
        center, slopes[:, :, 1:-1], padded[:, :, 3:-1], slopes[:, :, 2:], north_courant[None]
    )
    south = face_flux(
        padded[:, :, 1:-3], slopes[:, :, :-2], center, slopes[:, :, 1:-1], south_courant[None]
    )
    eastern = jnp.roll(center, -1, axis=3)
    western = jnp.roll(center, 1, axis=3)
    slope_x = min_mod(eastern - center, center - western)
    east = face_flux(center, slope_x, eastern, jnp.roll(slope_x, -1, axis=3), east_courant[None])
    west = jnp.roll(east, 1, axis=3)
    spacing = math.pi / total_rows
    row_float = global_rows.astype(jnp.float32)
    cos_north = jnp.sin((row_float + 1.0) * spacing)[:, None]
    cos_south = jnp.sin(row_float * spacing)[:, None]
    cos_center = jnp.sin((row_float + 0.5) * spacing)[:, None]
    return -(east - west) - (cos_north * north - cos_south * south) / cos_center


def make_basis(width):
    half_width = width // 2
    points = jnp.arange(width, dtype=jnp.int32)[:, None]
    column = jnp.arange(width, dtype=jnp.int32)[None, :]
    number = jnp.where(column <= half_width, column, column - half_width)
    phase = points * number % width
    angle = phase.astype(jnp.float32) * (2.0 * math.pi / width)
    basis = jnp.where(column <= half_width, jnp.cos(angle), jnp.sin(angle)).astype(jnp.bfloat16)
    flat_col = jnp.arange(width, dtype=jnp.int32)
    weights = jnp.where(
        (flat_col == 0) | (flat_col == half_width), 1.0 / width, 2.0 / width
    ).astype(jnp.float32)
    return (basis, weights)


def filter_block(band, index_rows, basis, weights, spectrum):
    fields, levels, count, width = band.shape
    one_hot = (
        index_rows[:, None] == jnp.arange(spectrum.shape[0], dtype=jnp.int32)[None, :]
    ).astype(jnp.float32)
    response = (
        jnp.dot(
            one_hot, spectrum, precision=lax.Precision.HIGHEST, preferred_element_type=jnp.float32
        )
        * weights[None, :]
    )
    flat = band.reshape(fields * levels * count, width)
    coefficients = jnp.dot(flat, basis, preferred_element_type=jnp.float32).reshape(
        fields, levels, count, width
    )
    scaled = (
        (coefficients * response[None, None])
        .astype(jnp.bfloat16)
        .reshape(fields * levels * count, width)
    )
    result = lax.dot_general(
        scaled, basis, (((1,), (1,)), ((), ())), preferred_element_type=jnp.float32
    )
    return result.reshape(fields, levels, count, width)


def on_device(tracers, east_courant, north_courant, spectrum, filter_index):
    lat_rows = tracers.shape[2]
    width = tracers.shape[3]
    devices = lax.axis_size("lon")
    device = lax.axis_index("lon")
    padded = extended(tracers, (("lon", 2),), 2)
    below_row = from_behind(north_courant[:, lat_rows - 1 :].astype(jnp.bfloat16), "lon", 1).astype(
        jnp.float32
    )
    south_courant = jnp.concatenate([below_row, north_courant[:, : lat_rows - 1]], axis=1)
    global_rows = device * lat_rows + jnp.arange(lat_rows, dtype=jnp.int32)
    increment = tendency(
        padded, south_courant, north_courant, east_courant, global_rows, lat_rows * devices
    )
    basis, weights = make_basis(width)
    quarter = devices // 4
    polar = (device < quarter) | (device >= devices - quarter)
    local_index = lax.dynamic_slice_in_dim(filter_index, device * lat_rows, lat_rows)
    return lax.cond(
        polar,
        lambda: tracers
        + filter_block(increment.astype(jnp.bfloat16), local_index, basis, weights, spectrum),
        lambda: tracers + increment,
    )


def solution(mesh):
    placed = (P("grp", None, "lon", None), P("grp", "lon", None), P("grp", "lon", None), P(), P())
    return jax.shard_map(
        on_device,
        mesh=mesh,
        in_specs=placed,
        out_specs=P("grp", None, "lon", None),
        check_vma=False,
    )
```

profile of v0, /device:TPU:1, one launch (start us, length us, event | category | flops | bytes accessed | tf_op | source)
XLA Modules:
  0.0 233.8 jit_solution(11522720221965324958)
XLA Ops:
  0.0 1.0 slice.133
  1.0 4.5 %collective-permute-start.2 = (bf16[4,1,2880]{2,1,0:T(2,128)(2,1)S(1)}, bf16[4,1,2880]{2,1,0:T(2,128)(2,1)S(1)}, u32[]{:S(2)}, u32[]{:S(2)}) collective-permute-start(bf16[4,1,2880]{2,1,0:T(2,128)(2,1)S(1)} %slice.133), channel_id=1, source_target_pairs={{0,1},{1,2},{2,3},{3,4},{4,5},{5,6},{6,7},{7,8},{8,9},{9,10},{10,1... | collective-permute-start | bytes 69128 | tf_op jit(solution)/shard_map/ppermute | solution.py:25
  5.6 3.2 %fusion.44 = (f32[5,4,2,2880]{3,2,1,0:T(2,128)S(1)}, f32[5,4,2,2880]{3,2,1,0:T(2,128)}) fusion(f32[5,4,16,2880]{3,2,1,0:T(8,128)} %param.7), kind=kLoop, calls=%fused_computation.76 | loop fusion | bytes 1843200 | tf_op jit(solution)/shard_map/slice | solution.py:17
  8.8 1.9 collective-permute-start
  10.7 3.6 %collective-permute-start.1 = (f32[5,4,2,2880]{3,2,1,0:T(2,128)}, f32[5,4,2,2880]{3,2,1,0:T(2,128)}, u32[]{:S(2)}, u32[]{:S(2)}) collective-permute-start(f32[5,4,2,2880]{3,2,1,0:T(2,128)} %get-tuple-element.96), channel_id=1, source_target_pairs={{0,1},{1,2},{2,3},{3,4},{4,5},{5,6},{6,7},{7,8},{8,9},{9,10},{10,1... | collective-permute-start | bytes 1382408 | tf_op jit(solution)/shard_map/ppermute | solution.py:14
  14.4 1.1 fusion.43
  15.5 2.6 %broadcast_maximum_fusion.1 = (f32[4,16,2880]{2,1,0:T(8,128)S(1)}, f32[4,16,2880]{2,1,0:T(8,128)}, f32[4,16,2880]{2,1,0:T(8,128)}, f32[4,16,2880]{2,1,0:T(8,128)}) fusion(f32[4,16,2880]{2,1,0:T(8,128)} %param.9), kind=kLoop, calls=%fused_computation.62 | loop fusion | flops 1105920 | bytes 3686400 | tf_op jit(solution)/shard_map/max | solution.py:33
  18.1 4.5 %fusion.42 = (f32[5,4,16,2879]{3,2,1,0:T(8,128)S(1)}, f32[5,4,16,2879]{3,2,1,0:T(8,128)S(1)}) fusion(f32[5,4,16,2880]{3,2,1,0:T(8,128)} %param.7), kind=kLoop, calls=%fused_computation.74 | loop fusion | bytes 14740480 | tf_op jit(solution)/shard_map/jit(_roll_static)/slice | solution.py:47
  22.6 4.6 %minimum_add_fusion.1 = f32[5,4,16,2880]{3,2,1,0:T(8,128)S(1)} fusion(f32[5,4,16,2880]{3,2,1,0:T(8,128)} %param.7, f32[5,4,16,2879]{3,2,1,0:T(8,128)S(1)} %get-tuple-element.92, f32[5,4,16,1]{3,2,1,0:T(8,128)S(1)} %get-tuple-element.94, f32[5,4,16,1]{3,2,1,0:T(8,128)S(1)} %get-tuple-element.93, f32[5,4,16,2879]{3,2,1,0:T(8,128)S(1)} %get-tuple-element.91), kind=kLoop, calls=%fused_computation.51 | loop fusion | flops 8294400 | bytes 14745600 | tf_op jit(solution)/shard_map/add | solution.py:29
  27.2 1.8 copy-done
  29.0 2.9 %slice.85 = f32[5,4,16,2879]{3,2,1,0:T(8,128)} slice(f32[5,4,16,2880]{3,2,1,0:T(8,128)S(1)} %minimum_add_fusion.1), slice={[0:5], [0:4], [0:16], [1:2880]} | slice | bytes 7370240 | tf_op jit(solution)/shard_map/jit(_roll_static)/slice | solution.py:50
  31.9 0.1 multiply_sine_fusion
  32.0 0.2 broadcast_maximum_fusion.2
  32.2 144.6 %select_convert_fusion = bf16[2880,2880]{1,0:T(8,128)(2,1)} fusion(s32[2880]{0:T(1024)S(1)} %add_select_fusion.1, pred[2880]{0:T(1024)(128)(4,1)S(1)} %iota_compare_fusion.2), kind=kLoop, calls=%fused_computation.16 | loop fusion | flops 91238400 | bytes 16603200 | tf_op jit(solution)/shard_map/convert_element_type | solution.py:67
  176.8 5.6 %fusion.40 = (f32[5,4,16,2880]{3,2,1,0:T(8,128)}, f32[5,4,18,2880]{3,2,1,0:T(8,128)}) fusion(f32[5,4,16,1]{3,2,1,0:T(8,128)S(1)} %slice.86, f32[5,4,16,2879]{3,2,1,0:T(8,128)S(1)} %copy-done.5, f32[5,4,16,2880]{3,2,1,0:T(8,128)} %param.7, f32[5,4,16,2880]{3,2,1,0:T(8,128)S(1)} %copy-done.1, f32[5,4,16,1]{3,2,1,0:T(8,128)S(1)} %get-tuple-element.93, ...), kind=kLoop, calls=%fused_computation.48 | loop fusion | flops 8294399 | bytes 25231360 | tf_op jit(solution)/shard_map/add | solution.py:33
  182.5 1.7 slice.87
  184.2 1.9 broadcast_maximum_fusion
  186.1 1.0 constant_dynamic-update-slice_fusion
  187.1 8.2 %minimum_add_fusion = f32[5,4,18,2880]{3,2,1,0:T(8,128)} fusion(f32[5,4,18,2880]{3,2,1,0:T(8,128)} %constant_dynamic-update-slice_fusion, f32[5,4,2,2880]{3,2,1,0:T(2,128)S(1)} %collective-permute-done, f32[5,4,16,2880]{3,2,1,0:T(8,128)} %param.7, f32[5,4,2,2880]{3,2,1,0:T(2,128)} %collective-permute-done.1), kind=kLoop, calls=%fused_computation.28 | loop fusion | flops 10368000 | bytes 12902400 | tf_op jit(solution)/shard_map/add | solution.py:29
  195.3 14.9 %fusion.33 = f32[5,4,16,2880]{3,2,1,0:T(8,128)} fusion(f32[5,4,16,2880]{3,2,1,0:T(8,128)} %param.7, f32[5,4,2,2880]{3,2,1,0:T(2,128)} %collective-permute-done.1, f32[5,4,18,2880]{3,2,1,0:T(8,128)} %minimum_add_fusion, f32[5,4,18,2880]{3,2,1,0:T(8,128)} %constant_dynamic-update-slice_fusion, f32[5,4,16,2880]{3,2,1,0:T(8,128)S(1)} %copy-done.2, ...), kind=kLoop, calls=%fused_computation.36 | loop fusion | flops 21196800 | bytes 35850432 | tf_op jit(solution)/shard_map/sub | solution.py:57
  210.2 23.5 %conditional.1 = (f32[5,4,16,2880]{3,2,1,0:T(8,128)}) conditional(s32[]{:T(128)} %convert_element_type.39, (f32[5,4,16,2880]{3,2,1,0:T(8,128)}, f32[5,4,16,2880]{3,2,1,0:T(8,128)}) %tuple.25, (f32[5,4,16,2880]{3,2,1,0:T(8,128)}, bf16[2880,2880]{1,0:T(8,128)(2,1)}, s32[]{:T(128)}, s32[256]{0:T(256)S(1)}, f32[64,2880]{1,0:T(8,128)}, ...), branch_computations={%region_0.1_spmd, %region_1.2_spmd} | conditional | flops 10655966208 | bytes 45377520 | solution.py:119
  210.2 0.1 dynamic_slice.4
  210.3 1.5 convolution_multiply_fusion
  211.8 21.9 %fusion.7 = f32[5,4,16,2880]{3,2,1,0:T(8,128)} fusion(f32[5,4,16,2880]{3,2,1,0:T(8,128)} %get-tuple-element.76, bf16[2880,2880]{1,0:T(8,128)(2,1)} %get-tuple-element.83, bf16[2880,2880]{1,0:T(8,128)(2,1)} %get-tuple-element.83, f32[16,2880]{1,0:T(8,128)S(1)} %convolution_multiply_fusion, f32[5,4,16,2880]{3,2,1,0:T(8,128)} %get-tuple-element.77), kind=kOutput, calls=%fused_computation.5 | convolution fusion | flops 10620518400 | bytes 44421120 | tf_op jit(solution)/shard_map/cond/branch_1_fun/dot_general | solution.py:95
  (27 shorter events, 0.2 us)
Async XLA Ops:
  1.0 183.1 %collective-permute-start.2 = (bf16[4,1,2880]{2,1,0:T(2,128)(2,1)S(1)}, bf16[4,1,2880]{2,1,0:T(2,128)(2,1)S(1)}, u32[]{:S(2)}, u32[]{:S(2)}) collective-permute-start(bf16[4,1,2880]{2,1,0:T(2,128)(2,1)S(1)} %slice.133), channel_id=1, source_target_pairs={{0,1},{1,2},{2,3},{3,4},{4,5},{5,6},{6,7},{7,8},{8,9},{9,10},{10,1... | collective-permute-start | bytes 69128 | tf_op jit(solution)/shard_map/ppermute | solution.py:25
  8.8 177.3 %collective-permute-start = (f32[5,4,2,2880]{3,2,1,0:T(2,128)S(1)}, f32[5,4,2,2880]{3,2,1,0:T(2,128)S(1)}, u32[]{:S(2)}, u32[]{:S(2)}) collective-permute-start(f32[5,4,2,2880]{3,2,1,0:T(2,128)S(1)} %get-tuple-element.95), channel_id=1, source_target_pairs={{1,0},{2,1},{3,2},{4,3},{5,4},{6,5},{7,6},{8,7},{9,8},{10,9},{11,1... | collective-permute-start | bytes 1382408 | tf_op jit(solution)/shard_map/ppermute | solution.py:17
  10.7 176.4 %collective-permute-start.1 = (f32[5,4,2,2880]{3,2,1,0:T(2,128)}, f32[5,4,2,2880]{3,2,1,0:T(2,128)}, u32[]{:S(2)}, u32[]{:S(2)}) collective-permute-start(f32[5,4,2,2880]{3,2,1,0:T(2,128)} %get-tuple-element.96), channel_id=1, source_target_pairs={{0,1},{1,2},{2,3},{3,4},{4,5},{5,6},{6,7},{7,8},{8,9},{9,10},{10,1... | collective-permute-start | bytes 1382408 | tf_op jit(solution)/shard_map/ppermute | solution.py:14
  22.6 4.6 %copy-start.3 = (f32[5,4,16,2879]{3,2,1,0:T(8,128)}, f32[5,4,16,2879]{3,2,1,0:T(8,128)S(1)}, u32[]{:S(2)}) copy-start(f32[5,4,16,2879]{3,2,1,0:T(8,128)S(1)} %get-tuple-element.91) | copy-start | bytes 11055364
  27.2 1.8 copy-start
  29.0 3.0 %copy-start.7 = (f32[4,16,2880]{2,1,0:T(8,128)S(1)}, f32[4,16,2880]{2,1,0:T(8,128)}, u32[]{:S(2)}) copy-start(f32[4,16,2880]{2,1,0:T(8,128)} %param.8) | copy-start | bytes 2211844
  32.2 144.6 %copy-start.1 = (f32[5,4,16,2880]{3,2,1,0:T(8,128)S(1)}, f32[5,4,16,2880]{3,2,1,0:T(8,128)}, u32[]{:S(2)}) copy-start(f32[5,4,16,2880]{3,2,1,0:T(8,128)} %copy-done) | copy-start | bytes 11059204
  32.2 144.6 %copy-start.4 = (f32[5,4,16,2879]{3,2,1,0:T(8,128)S(1)}, f32[5,4,16,2879]{3,2,1,0:T(8,128)}, u32[]{:S(2)}) copy-start(f32[5,4,16,2879]{3,2,1,0:T(8,128)} %copy-done.3) | copy-start | bytes 11055364
  32.2 144.6 %copy-start.5 = (f32[5,4,16,2879]{3,2,1,0:T(8,128)S(1)}, f32[5,4,16,2879]{3,2,1,0:T(8,128)}, u32[]{:S(2)}) copy-start(f32[5,4,16,2879]{3,2,1,0:T(8,128)} %slice.85) | copy-start | bytes 11055364
  176.8 7.4 %copy-start.6 = (f32[4,16,2880]{2,1,0:T(8,128)S(1)}, f32[4,16,2880]{2,1,0:T(8,128)}, u32[]{:S(2)}) copy-start(f32[4,16,2880]{2,1,0:T(8,128)} %param.9) | copy-start | bytes 2211844
  187.1 8.2 %copy-start.2 = (f32[5,4,16,2880]{3,2,1,0:T(8,128)S(1)}, f32[5,4,16,2880]{3,2,1,0:T(8,128)}, u32[]{:S(2)}) copy-start(f32[5,4,16,2880]{3,2,1,0:T(8,128)} %get-tuple-element.89) | copy-start | bytes 11059204
  195.3 14.9 %copy-start.8 = (s32[256]{0:T(256)S(1)}, s32[256]{0:T(256)}, u32[]{:S(2)}) copy-start(s32[256]{0:T(256)} %param.11) | copy-start | bytes 3076
where the time goes:
time: 234 us
  other arithmetic  183 us (78%)
  matrix products  23.4 us (10%)
  local copies, waits for them, and re-layouts  17.4 us (7%)
  starting transfers between devices  10.1 us (4%)
    convert_element_type x1, other arithmetic, make_basis(): jnp.where(column <= half_width, jnp.cos(angle), jnp.sin(angle))  145 us
    dot_general x1, matrix products, filter_block(): lax.dot_general(scaled, basis, (((1,), (1,)), ((), ())), preferred_elemen...  21.9 us
    sub x1, other arithmetic, tendency(): return -(east - west) - (cos_north * north - cos_south * south) / cos_center  14.9 us
    add x2, other arithmetic, min_mod(): jnp.maximum(jnp.minimum(left, right), 0.0)  12.8 us
    add x1, other arithmetic, face_flux(): jnp.maximum(courant, 0.0) * (left_q + 0.5 * (1.0 - courant) * left_s)  5.62 us
    slice x2, local copies, waits for them, and re-layouts, tendency(): eastern = jnp.roll(center, -1, axis=3)  5.6 us
  transfers between devices with their start and end apart: 3, of which 0 were waited for; matrix products, arithmetic and copies ran while one was open for 74% of the time, Pallas kernels for 0%

commit v1 on v0

v1 whole, which is shorter than its diff:
```python
import functools
import math

import jax
import jax.numpy as jnp
import ml_dtypes
import numpy as np
from jax import lax
from jax.experimental import pallas as pl
from jax.experimental.pallas import tpu as pltpu
from jax.sharding import PartitionSpec as P

LANES = 128
CHUNK = 256


def up_to(value, multiple):
    return -(-value // multiple) * multiple


def column_groups(width):
    half = width // 2
    column = np.arange(width)
    number = np.where(column <= half, column, column - half)
    return number, [np.where(number % 4 == 0)[0], np.where(number % 4 == 2)[0], np.where(number % 2 == 1)[0]]


def make_matrices(width):
    half, part = width // 2, width // 4
    deep = up_to(part, CHUNK)
    number, groups = column_groups(width)
    points = np.arange(half, dtype=np.int64)[:, None]
    angle = ((points * number[None, :]) % width) * (2.0 * math.pi / width)
    basis = np.where(np.arange(width)[None, :] <= half, np.cos(angle), np.sin(angle))
    even = np.zeros((2, deep, deep), np.float64)
    for at in range(2):
        even[at, :part, : len(groups[at])] = basis[:part, groups[at]]
    odd = np.zeros((2, deep, 2 * deep), np.float64)
    odd[0, :part, : len(groups[2])] = basis[:part, groups[2]]
    odd[1, :part, : len(groups[2])] = basis[part:, groups[2]]
    odd = odd.reshape(2 * deep, 2 * deep)
    kind = ml_dtypes.bfloat16
    return (
        even.astype(kind),
        odd.astype(kind),
        np.ascontiguousarray(even.transpose(0, 2, 1)).astype(kind),
        np.ascontiguousarray(odd.T).astype(kind),
    )


def min_mod(a, b):
    return jnp.maximum(jnp.minimum(a, jnp.maximum(b, 0.0)), jnp.minimum(b, 0.0))


def upwind(c, ch, ql, sl, qr, sr):
    ahead = c > 0.0
    return c * jnp.where(ahead, ql, qr) + ch * jnp.where(ahead, sl, sr)


def second(c):
    return c * (jnp.where(c > 0.0, 0.5, -0.5) - 0.5 * c)


def kernel(width, polar_ref, q_ref, ce_ref, cn_ref, cs_ref, halo_ref, ratio_ref, resp_ref,
           even_hbm, odd_hbm, even_t_hbm, odd_t_hbm, out_ref,
           che_s, chn_s, inc_s, y_s, s_s, even_s, odd_s, even_t_s, odd_t_s, sems):
    planes, rows, _ = q_ref.shape
    levels = ce_ref.shape[0]
    part = width // 4
    deep = up_to(part, CHUNK)
    full = width // LANES
    rest = width - full * LANES
    tiles = full + (1 if rest else 0)
    lane = lax.broadcasted_iota(jnp.int32, (rows, LANES), 1)
    row = lax.broadcasted_iota(jnp.int32, (rows, LANES), 0)
    copies = [
        pltpu.make_async_copy(source, target, sems.at[at])
        for at, (source, target) in enumerate(
            ((even_hbm, even_s), (odd_hbm, odd_s), (even_t_hbm, even_t_s), (odd_t_hbm, odd_t_s))
        )
    ]
    polar = polar_ref[0] == 1

    @pl.when(polar)
    def _():
        for copy in copies:
            copy.start()

    def tile_of(ref, at, t):
        if t < full:
            return ref[at, :, LANES * t : LANES * (t + 1)]
        return jnp.concatenate(
            [ref[at, :, LANES * full : width], ref[at, :, : LANES - rest]], axis=1
        )

    def prepare(level, carry):
        for t in range(tiles):
            che_s[level, :, LANES * t : LANES * (t + 1)] = second(tile_of(ce_ref, level, t))
            chn_s[level, :, LANES * t : LANES * (t + 1)] = second(tile_of(cn_ref, level, t))
        return carry

    lax.fori_loop(0, levels, prepare, 0)

    def increments(p, level, put):
        memo = {}

        def cached(function):
            def call(t):
                key = (function.__name__, t)
                if key not in memo:
                    memo[key] = function(t)
                return memo[key]

            return call

        def wrapped(load, t):
            if t >= 0:
                return load(min(t, tiles - 1))
            return pltpu.roll(load(tiles - 1), LANES - rest, 1) if rest else load(tiles - 1)

        @cached
        def q(t):
            return wrapped(lambda k: tile_of(q_ref, p, k), t)

        @cached
        def q_left(t):
            return pltpu.roll(q(t), LANES - 1, 1)

        @cached
        def q_east(t):
            return jnp.where(lane == LANES - 1, q_left(min(t + 1, tiles - 1)), q_left(t))

        @cached
        def d(t):
            return q_east(t) - q(t)

        @cached
        def d_right(t):
            return pltpu.roll(d(t), 1, 1)

        @cached
        def s(t):
            return min_mod(d(t), jnp.where(lane == 0, d_right(max(t - 1, -1)), d_right(t)))

        @cached
        def s_left(t):
            return pltpu.roll(s(t), LANES - 1, 1)

        @cached
        def east(t):
            s_east = jnp.where(lane == LANES - 1, s_left(min(t + 1, tiles - 1)), s_left(t))
            c = wrapped(lambda k: tile_of(ce_ref, level, k), t)
            ch = wrapped(lambda k: che_s[level, :, LANES * k : LANES * (k + 1)], t)
            return upwind(c, ch, q(t), s(t), q_east(t), s_east)

        @cached
        def east_right(t):
            return pltpu.roll(east(t), 1, 1)

        rn, rs = ratio_ref[0], ratio_ref[1]
        for t in range(tiles):
            inc_x = jnp.where(lane == 0, east_right(t - 1), east_right(t)) - east(t)
            here = q(t)
            halo = tile_of(halo_ref, p, t)
            low0, low1, high0, high1 = (halo[k : k + 1] for k in range(4))
            cn = tile_of(cn_ref, level, t)
            chn = chn_s[level, :, LANES * t : LANES * (t + 1)]
            cs = tile_of(cs_ref, level, t)
            q_north = jnp.where(row == rows - 1, high0, pltpu.roll(here, rows - 1, 0))
            dy = q_north - here
            dy_low = here[0:1] - low1
            sy = min_mod(dy, jnp.where(row == 0, dy_low, pltpu.roll(dy, 1, 0)))
            sy_high = min_mod(high1 - high0, dy[rows - 1 : rows])
            sy_north = jnp.where(row == rows - 1, sy_high, pltpu.roll(sy, rows - 1, 0))
            north = upwind(cn, chn, here, sy, q_north, sy_north)
            sy_low = min_mod(dy_low, low1 - low0)
            south_row = upwind(cs, second(cs), low1, sy_low, here[0:1], sy[0:1])
            south = jnp.where(row == 0, south_row, pltpu.roll(north, 1, 0))
            put(t, here, inc_x + (rs * south - rn * north))

    @pl.when(jnp.logical_not(polar))
    def _():
        def plane(p, carry):
            def put(t, here, inc):
                size = LANES if t < full else rest
                out_ref[p, :, LANES * t : LANES * t + size] = (here + inc)[:, :size]

            increments(p, lax.rem(p, levels), put)
            return carry

        lax.fori_loop(0, planes, plane, 0)

    @pl.when(polar)
    def _():
        def plane(p, carry):
            def put(t, here, inc):
                if t >= full:
                    inc = jnp.where(lane < rest, inc, 0.0)
                inc_s[:, LANES * t : LANES * (t + 1)] = inc

            increments(p, lax.rem(p, levels), put)
            x0, x1, x2, x3 = (inc_s[:, part * k : part * k + deep] for k in range(4))
            a, b = x0 + x2, x1 + x3
            where = pl.ds(pl.multiple_of(p * rows, rows), rows)
            for k, y in enumerate((a + b, a - b, x0 - x2, x1 - x3)):
                y_s[where, deep * k : deep * (k + 1)] = y.astype(jnp.bfloat16)
            return carry

        lax.fori_loop(0, planes, plane, 0)
        total = planes * rows

        def forward(y, matrix, at):
            coefficients = jnp.dot(y, matrix, preferred_element_type=jnp.float32)
            scaled = coefficients.reshape(planes, rows, CHUNK) * resp_ref[:, at : at + CHUNK][None]
            s_s[:, at : at + CHUNK] = scaled.reshape(total, CHUNK).astype(jnp.bfloat16)

        copies[0].wait()
        for k in range(2):
            for n in range(deep // CHUNK):
                forward(
                    y_s[:, deep * k : deep * (k + 1)],
                    even_s[k, :, CHUNK * n : CHUNK * (n + 1)],
                    deep * k + CHUNK * n,
                )
        copies[1].wait()
        for n in range(2 * deep // CHUNK):
            forward(
                y_s[:, 2 * deep :], odd_s[:, CHUNK * n : CHUNK * (n + 1)], 2 * deep + CHUNK * n
            )
        copies[2].wait()
        copies[3].wait()
        for n in range(deep // CHUNK):
            span = slice(CHUNK * n, CHUNK * (n + 1))
            size = min(CHUNK, part - CHUNK * n)

            def back(scaled, matrix):
                return jnp.dot(scaled, matrix, preferred_element_type=jnp.float32)

            e0 = back(s_s[:, :deep], even_t_s[0, :, span])
            e2 = back(s_s[:, deep : 2 * deep], even_t_s[1, :, span])
            eu = back(s_s[:, 2 * deep :], odd_t_s[:, span])
            ev = back(s_s[:, 2 * deep :], odd_t_s[:, deep + CHUNK * n : deep + CHUNK * (n + 1)])
            plus, minus = e0 + e2, e0 - e2
            for k, value in enumerate((plus + eu, minus + ev, plus - eu, minus - ev)):
                start = part * k + CHUNK * n
                out_ref[:, :, start : start + size] = (
                    q_ref[:, :, start : start + size]
                    + value.reshape(planes, rows, CHUNK)[:, :, :size]
                )


def shifted(x, axis, by):
    count = lax.axis_size(axis)
    return lax.ppermute(x, axis, [(i, i + by) for i in range(count) if 0 <= i + by < count])


def on_device(tracers, east_courant, north_courant, spectrum, filter_index):
    fields, levels, rows, width = tracers.shape
    planes = fields * levels
    devices = lax.axis_size("lon")
    device = lax.axis_index("lon")
    part = width // 4
    deep = up_to(part, CHUNK)
    wide = up_to(width, LANES)
    q = tracers.reshape(planes, rows, width)
    kind = jnp.bfloat16
    up = jnp.concatenate(
        [
            q[:, rows - 2 :].astype(kind).reshape(2 * planes, width),
            north_courant[:, rows - 1].astype(kind),
        ],
        axis=0,
    )
    low = shifted(up, "lon", 1)
    high = shifted(q[:, :2].astype(kind).reshape(2 * planes, width), "lon", -1)
    halo = jnp.concatenate(
        [low[: 2 * planes].reshape(planes, 2, width), high.reshape(planes, 2, width)], axis=1
    ).astype(jnp.float32)
    south_courant = low[2 * planes :].astype(jnp.float32).reshape(levels, 1, width)
    spacing = math.pi / (rows * devices)
    where = (device * rows + jnp.arange(rows, dtype=jnp.int32)).astype(jnp.float32)
    center = jnp.sin((where + 0.5) * spacing)
    ratio = jnp.stack([jnp.sin((where + 1.0) * spacing) / center, jnp.sin(where * spacing) / center])
    ratio = jnp.broadcast_to(ratio[:, :, None], (2, rows, LANES))
    quarter = devices // 4
    polar = ((device < quarter) | (device >= devices - quarter)).astype(jnp.int32).reshape(1)
    half = width // 2
    chosen = jnp.take(spectrum, lax.dynamic_slice_in_dim(filter_index, device * rows, rows), axis=0)
    column = np.arange(width)
    weight = np.where((column == 0) | (column == half), 1.0 / width, 2.0 / width).astype(np.float32)
    chosen = chosen * weight[None, :]
    zeros = jnp.zeros((rows, deep - part), jnp.float32)
    response = jnp.concatenate(
        [
            chosen[:, 0 : half + 1 : 4], chosen[:, half + 4 :: 4], zeros,
            chosen[:, 2 : half + 1 : 4], chosen[:, half + 2 :: 4], zeros,
            chosen[:, 1 : half + 1 : 2], chosen[:, half + 1 :: 2], zeros, zeros,
        ],
        axis=1,
    )
    matrices = [jnp.asarray(m) for m in make_matrices(width)]
    vmem = pl.BlockSpec(memory_space=pltpu.VMEM)
    out = pl.pallas_call(
        functools.partial(kernel, width),
        out_shape=jax.ShapeDtypeStruct(q.shape, jnp.float32),
        in_specs=[pl.BlockSpec(memory_space=pltpu.SMEM)] + [vmem] * 7 + [pl.BlockSpec(memory_space=pl.ANY)] * 4,
        out_specs=vmem,
        scratch_shapes=[
            pltpu.VMEM((levels, rows, wide), jnp.float32),
            pltpu.VMEM((levels, rows, wide), jnp.float32),
            pltpu.VMEM((rows, 3 * part + deep + LANES), jnp.float32),
            pltpu.VMEM((planes * rows, 4 * deep), kind),
            pltpu.VMEM((planes * rows, 4 * deep), kind),
        ]
        + [pltpu.VMEM(m.shape, kind) for m in matrices]
        + [pltpu.SemaphoreType.DMA((4,))],
        compiler_params=pltpu.CompilerParams(vmem_limit_bytes=56 * 2**20),
    )(polar, q, east_courant, north_courant, south_courant, halo, ratio, response, *matrices)
    return out.reshape(tracers.shape)


def solution(mesh):
    placed = (P("grp", None, "lon", None), P("grp", "lon", None), P("grp", "lon", None), P(), P())
    return jax.shard_map(
        on_device,
        mesh=mesh,
        in_specs=placed,
        out_specs=P("grp", None, "lon", None),
        check_vma=False,
    )
```

time: 234 us -> 44.8 us (0.19)
  other arithmetic: 183 us -> 4 us
  matrix products: 23.4 us -> 0 us
  Pallas kernels: 0 us -> 22.6 us
  local copies, waits for them, and re-layouts: 17.4 us -> 11.2 us
  starting transfers between devices: 10.1 us -> 6.46 us
    convert_element_type x2 -> x1, other arithmetic: 145 us -> 1.38 us  [on_device(): halo = jnp.concatenate([low[:2 * planes].reshape(planes, 2, width), high....]
    dot_general x2 -> x0, matrix products: 23.4 us -> none  [the longest x1 21.9 us: filter_block(): lax.dot_general(scaled, basis, (((1,), (1,)), ((), ())), preferred_elemen...]
    pallas_call x0 -> x1, Pallas kernels: none -> 22.6 us  [on_device(): pl.pallas_call(functools.partial(kernel, width), out_shape=jax.ShapeDtype...]
    add x3 -> x0, other arithmetic: 18.4 us -> none  [the longest x2 12.8 us: min_mod(): jnp.maximum(jnp.minimum(left, right), 0.0)]
    sub x1 -> x0, other arithmetic: 14.9 us -> none  [tendency(): return -(east - west) - (cos_north * north - cos_south * south) / cos_center]
    slice x7 -> x9, local copies, waits for them, and re-layouts: 14.4 us -> 7.88 us  [the longest x1 1.58 us: on_device(): chosen[:, 1:half + 1:2]]
    max x3 -> x0, other arithmetic: 4.64 us -> none  [face_flux(): jnp.maximum(courant, 0.0) * (left_q + 0.5 * (1.0 - courant) * left_s)]
    ppermute x3 -> x2, starting transfers between devices: 10.1 us -> 6.46 us  [shifted(): lax.ppermute(x, axis, [(i, i + by) for i in range(count) if 0 <= i + by <...]
  transfers between devices with their start and end apart: 3 -> 2, of which waited for: 0 -> 0; matrix products, arithmetic and copies ran while one was open for 74% -> 21% of each run, Pallas kernels for 0% -> 0%
where the time goes in v1:
time: 44.8 us; the launch traced here: 44.6 us
  Pallas kernels  22.6 us (50%)
  local copies, waits for them, and re-layouts  11.2 us (25%)
  starting transfers between devices  6.46 us (14%)
  other arithmetic  4 us (9%)
    pallas_call x1, Pallas kernels, on_device(): pl.pallas_call(functools.partial(kernel, width), out_shape=jax.ShapeDtype...  22.6 us
    ppermute x2, starting transfers between devices, shifted(): lax.ppermute(x, axis, [(i, i + by) for i in range(count) if 0 <= i + by <...  6.46 us
    another operation x1, other arithmetic  2.34 us
    slice x1, local copies, waits for them, and re-layouts, on_device(): chosen[:, 1:half + 1:2]  1.58 us
    slice x1, local copies, waits for them, and re-layouts, on_device(): chosen[:, half + 1::2]  1.58 us
    convert_element_type x1, other arithmetic, on_device(): halo = jnp.concatenate([low[:2 * planes].reshape(planes, 2, width), high....  1.38 us
    slice x1, local copies, waits for them, and re-layouts, on_device(): north_courant[:, rows - 1].astype(kind)  1.04 us
  transfers between devices with their start and end apart: 2, of which 0 were waited for; matrix products, arithmetic and copies ran while one was open for 21% of the time, Pallas kernels for 0%

profile of v1, /device:TPU:1, one launch (start us, length us, event | category | flops | bytes accessed | tf_op | source)
XLA Modules:
  0.0 44.6 jit_solution(9769891031098869316)
XLA Ops:
  0.0 2.3 %bitcast_convert_fusion = bf16[20,16,2880]{2,1,0:T(8,128)(2,1)S(1)} fusion(f32[5,4,16,2880]{3,2,1,0:T(8,128)} %param.10), kind=kLoop, calls=%fused_computation.15 | loop fusion | flops 921600 | bytes 5529600 | tf_op jit(solution)/shard_map/convert.4
  2.4 0.4 fusion.1
  2.7 0.2 reshape.83
  2.9 2.0 %collective-permute-start.1 = (bf16[40,2880]{1,0:T(8,128)(2,1)S(1)}, bf16[40,2880]{1,0:T(8,128)(2,1)S(1)}, u32[]{:S(2)}, u32[]{:S(2)}) collective-permute-start(bf16[40,2880]{1,0:T(8,128)(2,1)S(1)} %reshape.83), channel_id=1, source_target_pairs={{1,0},{2,1},{3,2},{4,3},{5,4},{6,5},{7,6},{8,7},{9,8},{10,9},{11,1... | collective-permute-start | bytes 691208 | tf_op jit(solution)/shard_map/ppermute | solution.py:254
  4.9 1.0 %slice.50 = bf16[4,1,2880]{2,1,0:T(2,128)(2,1)S(1)} slice(f32[4,16,2880]{2,1,0:T(8,128)} %cn_ref.1), slice={[0:4], [15:16], [0:2880]} | slice | bytes 46080 | tf_op jit(solution)/shard_map/slice | solution.py:270
  5.9 0.2 reshape.79
  6.2 4.5 %collective-permute-start = (bf16[44,2880]{1,0:T(8,128)(2,1)S(1)}, bf16[44,2880]{1,0:T(8,128)(2,1)S(1)}, u32[]{:S(2)}, u32[]{:S(2)}) collective-permute-start(bf16[44,2880]{1,0:T(8,128)(2,1)S(1)} %pad_maximum_fusion), channel_id=1, source_target_pairs={{0,1},{1,2},{2,3},{3,4},{4,5},{5,6},{6,7},{7,8},{8,9},{9,10},{10,1... | collective-permute-start | bytes 760328 | tf_op jit(solution)/shard_map/ppermute | solution.py:254
  10.7 0.1 compare_and_fusion
  10.8 0.6 %gather_fusion = f32[16,2880]{1,0:T(8,128)S(1)} fusion(f32[64,2880]{1,0:T(8,128)S(1)} %copy-done, s32[1024]{0:T(1024)S(1)} %pad_clamp_fusion), kind=kCustom, calls=%fused_computation | custom fusion | bytes 368704 | tf_op jit(solution)/shard_map/jit(_take)/gather | solution.py:288
  11.4 0.1 select_multiply_fusion
  11.5 0.8 %slice.44 = f32[16,360]{1,0:T(8,128)S(1)} slice(f32[16,2880]{1,0:T(8,128)S(1)} %select_multiply_fusion), slice={[0:16:1], [1442:2880:4]} | slice | bytes 46080 | tf_op jit(solution)/shard_map/slice | solution.py:296
  12.3 0.8 %slice.43 = f32[16,360]{1,0:T(8,128)S(1)} slice(f32[16,2880]{1,0:T(8,128)S(1)} %select_multiply_fusion), slice={[0:16:1], [2:1441:4]} | slice | bytes 46080 | tf_op jit(solution)/shard_map/slice | solution.py:296
  13.2 0.8 %slice.42 = f32[16,359]{1,0:T(8,128)S(1)} slice(f32[16,2880]{1,0:T(8,128)S(1)} %select_multiply_fusion), slice={[0:16:1], [1444:2880:4]} | slice | bytes 45952 | tf_op jit(solution)/shard_map/slice | solution.py:295
  14.0 0.8 %slice.41 = f32[16,361]{1,0:T(8,128)S(1)} slice(f32[16,2880]{1,0:T(8,128)S(1)} %select_multiply_fusion), slice={[0:16:1], [0:1441:4]} | slice | bytes 46208 | tf_op jit(solution)/shard_map/slice | solution.py:295
  14.8 1.6 %slice.46 = f32[16,720]{1,0:T(8,128)S(1)} slice(f32[16,2880]{1,0:T(8,128)S(1)} %select_multiply_fusion), slice={[0:16:1], [1441:2880:2]} | slice | bytes 92160 | tf_op jit(solution)/shard_map/slice | solution.py:297
  16.4 1.6 %slice.45 = f32[16,720]{1,0:T(8,128)S(1)} slice(f32[16,2880]{1,0:T(8,128)S(1)} %select_multiply_fusion), slice={[0:16:1], [1:1441:2]} | slice | bytes 92160 | tf_op jit(solution)/shard_map/slice | solution.py:297
  18.0 0.8 %concatenate.15.resp_ref = f32[16,3072]{1,0:T(8,128)} concatenate(f32[16,361]{1,0:T(8,128)S(1)} %slice.41, f32[16,359]{1,0:T(8,128)S(1)} %slice.42, f32[16,48]{1,0:T(8,128)S(1)} %broadcast_in_dim.25, f32[16,360]{1,0:T(8,128)S(1)} %slice.43, f32[16,360]{1,0:T(8,128)S(1)} %slice.44, f32[16,48]{1,0:T(8,128)S(1)} %broadcast_in_dim.25, f32[16,720]{1,0:T(8,128)S(1)} %slice.45, ...), dimensions={1} | concatenate | bytes 393216 | tf_op jit(solution)/shard_map/concatenate | solution.py:293
  18.8 0.1 sine_divide_fusion
  18.9 0.1 reshape.84
  19.0 0.1 reshape.82
  19.1 0.7 %reshape.89.cs_ref = f32[4,1,2880]{2,1,0:T(1,128)} reshape(f32[4,2880]{1,0:T(4,128)S(1)} %slice_convert_fusion) | data formatting | bytes 92160 | tf_op jit(solution)/shard_map/reshape | solution.py:279
  19.8 1.4 %maximum_convert_fusion.halo_ref = f32[20,4,2880]{2,1,0:T(4,128)} fusion(bf16[20,2,2880]{2,1,0:T(2,128)(2,1)S(1)} %reshape.84, bf16[20,2,2880]{2,1,0:T(2,128)(2,1)S(1)} %reshape.82), kind=kLoop, calls=%fused_computation.1 | loop fusion | flops 921600 | bytes 1382400 | tf_op jit(solution)/shard_map/convert_element_type | solution.py:278
  21.2 0.7 %broadcast_in_dim.21.ratio_ref = f32[2,16,128]{2,1,0:T(8,128)} broadcast(f32[2,16]{1,0:T(2,128)S(1)} %pad_maximum_fusion.1), dimensions={0,1} | broadcast | bytes 16512 | tf_op jit(solution)/shard_map/broadcast_in_dim | solution.py:284
  21.8 22.6 %shard_map.100 = f32[20,16,2880]{2,1,0:T(8,128)} custom-call(s32[1]{0:T(128)} %bitcast.polar_ref, f32[20,16,2880]{2,1,0:T(8,128)} %bitcast.7, f32[4,16,2880]{2,1,0:T(8,128)} %ce_ref.1, f32[4,16,2880]{2,1,0:T(8,128)} %cn_ref.1, f32[4,1,2880]{2,1,0:T(1,128)} %reshape.89.cs_ref, f32[20,4,2880]{2,1,0:T(4,128)} %maximum_convert_fusion.halo_ref, ...), custom_call_target="tpu_custom_call" | custom-call | tf_op jit(solution)/shard_map/pallas_call | solution.py:303
  (16 shorter events, 0.1 us)
Async XLA Ops:
  0.0 10.8 %copy-start = (f32[64,2880]{1,0:T(8,128)S(1)}, f32[64,2880]{1,0:T(8,128)}, u32[]{:S(2)}) copy-start(f32[64,2880]{1,0:T(8,128)} %param.13) | copy-start | bytes 2211844
  0.0 11.4 %copy-start.1 = (f32[2880]{0:T(1024)S(1)}, f32[2880]{0:T(1024)}, u32[]{:S(2)}) copy-start(f32[2880]{0:T(1024)} %constant.54) | copy-start | bytes 34564
  0.0 10.7 %copy-start.2 = (s32[256]{0:T(256)S(1)}, s32[256]{0:T(256)}, u32[]{:S(2)}) copy-start(s32[256]{0:T(256)} %param.14) | copy-start | bytes 3076
  2.9 16.0 %collective-permute-start.1 = (bf16[40,2880]{1,0:T(8,128)(2,1)S(1)}, bf16[40,2880]{1,0:T(8,128)(2,1)S(1)}, u32[]{:S(2)}, u32[]{:S(2)}) collective-permute-start(bf16[40,2880]{1,0:T(8,128)(2,1)S(1)} %reshape.83), channel_id=1, source_target_pairs={{1,0},{2,1},{3,2},{4,3},{5,4},{6,5},{7,6},{8,7},{9,8},{10,9},{11,1... | collective-permute-start | bytes 691208 | tf_op jit(solution)/shard_map/ppermute | solution.py:254
  6.2 12.8 %collective-permute-start = (bf16[44,2880]{1,0:T(8,128)(2,1)S(1)}, bf16[44,2880]{1,0:T(8,128)(2,1)S(1)}, u32[]{:S(2)}, u32[]{:S(2)}) collective-permute-start(bf16[44,2880]{1,0:T(8,128)(2,1)S(1)} %pad_maximum_fusion), channel_id=1, source_target_pairs={{0,1},{1,2},{2,3},{3,4},{4,5},{5,6},{6,7},{7,8},{8,9},{9,10},{10,1... | collective-permute-start | bytes 760328 | tf_op jit(solution)/shard_map/ppermute | solution.py:254

commit v2 on v1

--- a/solution.py
+++ b/solution.py
@@ -48,6 +48,121 @@
     )
 
 
+def make_order():
+    at = np.arange(CHUNK)
+    source = np.concatenate([at[at % 4 == 0], at[at % 4 == 2], at[at % 2 == 1]])
+    order = np.zeros((CHUNK, CHUNK), np.float32)
+    order[source, at] = 1.0
+    return order.astype(ml_dtypes.bfloat16)
+
+
+def exchange(count, q_hbm, cn_hbm, edge_ref, south_s, north_s, cn_s, packs, up_s, down_s, low_s, high_s,
+             local, send, recv):
+    planes, rows, width = q_hbm.shape
+    levels = cn_hbm.shape[0]
+    deep = edge_ref.shape[1]
+    me = lax.axis_index("lon")
+    last = count - 1
+    loads = [
+        pltpu.make_async_copy(q_hbm.at[:, pl.ds(rows - 8, 8), :], north_s, local.at[0]),
+        pltpu.make_async_copy(cn_hbm.at[:, pl.ds(rows - 8, 8), :], cn_s, local.at[1]),
+        pltpu.make_async_copy(q_hbm.at[:, pl.ds(0, 8), :], south_s, local.at[2]),
+    ]
+    for load in loads:
+        load.start()
+    barrier = pltpu.get_barrier_semaphore()
+
+    @pl.when(me > 0)
+    def _():
+        pl.semaphore_signal(barrier, inc=1, device_id={"lon": me - 1}, device_id_type=pl.DeviceIdType.MESH)
+
+    @pl.when(me < last)
+    def _():
+        pl.semaphore_signal(barrier, inc=1, device_id={"lon": me + 1}, device_id_type=pl.DeviceIdType.MESH)
+
+    for at in range(2):
+        packs[at, 2 * deep - levels :, :] = jnp.zeros((levels, width), jnp.float32)
+        packs[at, planes:deep, :] = jnp.zeros((levels, width), jnp.float32)
+
+    loads[0].wait()
+    loads[1].wait()
+    for p in range(planes):
+        packs[0, p : p + 1, :] = north_s[p, 6:7, :]
+        packs[0, deep + p : deep + p + 1, :] = north_s[p, 7:8, :]
+    for p in range(levels):
+        packs[0, planes + p : planes + p + 1, :] = cn_s[p, 7:8, :]
+    up_s[...] = packs[0].astype(jnp.bfloat16)
+
+    outer = jnp.logical_or(me == 0, me == last)
+
+    @pl.when(outer)
+    def _():
+        pl.semaphore_wait(barrier, 1)
+
+    @pl.when(jnp.logical_not(outer))
+    def _():
+        pl.semaphore_wait(barrier, 2)
+
+    up = pltpu.make_async_remote_copy(
+        src_ref=up_s, dst_ref=low_s, send_sem=send.at[0], recv_sem=recv.at[0],
+        device_id={"lon": me + 1}, device_id_type=pl.DeviceIdType.MESH,
+    )
+    down = pltpu.make_async_remote_copy(
+        src_ref=down_s, dst_ref=high_s, send_sem=send.at[1], recv_sem=recv.at[1],
+        device_id={"lon": me - 1}, device_id_type=pl.DeviceIdType.MESH,
+    )
+
+    @pl.when(me < last)
+    def _():
+        up.start()
+
+    loads[2].wait()
+    for p in range(planes):
+        packs[1, p : p + 1, :] = south_s[p, 0:1, :]
+        packs[1, deep + p : deep + p + 1, :] = south_s[p, 1:2, :]
+    down_s[...] = packs[1].astype(jnp.bfloat16)
+
+    @pl.when(me > 0)
+    def _():
+        down.start()
+        up.wait_recv()
+
+    @pl.when(me == 0)
+    def _():
+        low_s[...] = jnp.zeros_like(low_s)
+
+    @pl.when(me < last)
+    def _():
+        down.wait_recv()
+
+    @pl.when(me == last)
+    def _():
+        high_s[...] = jnp.zeros_like(high_s)
+
+    for start in range(0, width, LANES):
+        span = slice(start, min(start + LANES, width))
+        low = low_s[:, span].astype(jnp.float32)
+        high = high_s[:, span].astype(jnp.float32)
+        low0, low1, high0, high1 = low[:deep], low[deep:], high[:deep], high[deep:]
+        q0, q1, q_last = packs[1, :deep, span], packs[1, deep:, span], packs[0, deep:, span]
+        cs = jnp.concatenate([low[planes : planes + levels]] * (deep // levels), axis=0)
+        dy = q0 - low1
+        edge_ref[0, :, span] = upwind(
+            cs, second(cs), low1, min_mod(dy, low1 - low0), q0, min_mod(q1 - q0, dy)
+        )
+        edge_ref[1, :, span] = high0
+        edge_ref[2, :, span] = min_mod(high1 - high0, high0 - q_last)
+        edge_ref[3, :, span] = low1
+
+    @pl.when(me < last)
+    def _():
+        up.wait_send()
+
+    @pl.when(me > 0)
+    def _():
+        down.wait_send()
+
+
 def min_mod(a, b):
     return jnp.maximum(jnp.minimum(a, jnp.maximum(b, 0.0)), jnp.minimum(b, 0.0))
 
@@ -61,9 +176,10 @@
     return c * (jnp.where(c > 0.0, 0.5, -0.5) - 0.5 * c)
 
 
-def kernel(width, polar_ref, q_ref, ce_ref, cn_ref, cs_ref, halo_ref, ratio_ref, resp_ref,
-           even_hbm, odd_hbm, even_t_hbm, odd_t_hbm, out_ref,
-           che_s, chn_s, inc_s, y_s, s_s, even_s, odd_s, even_t_s, odd_t_s, sems):
+def kernel(width, count, where_ref, index_ref, q_hbm, ce_ref, cn_ref, edge_ref, spectrum_ref, order_ref,
+           even_hbm, odd_hbm, even_t_hbm, odd_t_hbm, out_hbm,
+           q_ref, out_ref, chosen_s, resp_ref, ratio_s, che_s, chn_s, inc_s, y_s, s_s,
+           even_s, odd_s, even_t_s, odd_t_s, sems, in_sems, out_sems):
     planes, rows, _ = q_ref.shape
     levels = ce_ref.shape[0]
     part = width // 4
@@ -79,12 +195,31 @@
             ((even_hbm, even_s), (odd_hbm, odd_s), (even_t_hbm, even_t_s), (odd_t_hbm, odd_t_s))
         )
     ]
-    polar = polar_ref[0] == 1
+    device = where_ref[0]
+    quarter = count // 4
+    polar = jnp.logical_or(device < quarter, device >= count - quarter)
+
+    def q_copy(p):
+        return pltpu.make_async_copy(q_hbm.at[p], q_ref.at[p], in_sems.at[p])
+
+    def out_copy(p):
+        return pltpu.make_async_copy(out_ref.at[p], out_hbm.at[p], out_sems.at[p])
+
+    def over_planes(act):
+        lax.fori_loop(0, planes, lambda p, carry: (act(p), carry)[1], 0)
+
+    over_planes(lambda p: q_copy(p).start())
 
     @pl.when(polar)
     def _():
         for copy in copies:
             copy.start()
+
+    spacing = math.pi / (rows * count)
+    place = (device * rows + row).astype(jnp.float32)
+    center = jnp.sin((place + 0.5) * spacing)
+    ratio_s[0] = jnp.sin((place + 1.0) * spacing) / center
+    ratio_s[1] = jnp.sin(place * spacing) / center
 
     def tile_of(ref, at, t):
         if t < full:
@@ -157,26 +292,77 @@
         def east_right(t):
             return pltpu.roll(east(t), 1, 1)
 
-        rn, rs = ratio_ref[0], ratio_ref[1]
+        rn, rs = ratio_s[0], ratio_s[1]
+
+        def edge(k, t, target):
+            at = pl.ds(pl.multiple_of(p // 8 * 8, 8), 8)
+            if t < full:
+                value = edge_ref[k, at, LANES * t : LANES * (t + 1)]
+            else:
+                value = jnp.concatenate(
+                    [edge_ref[k, at, LANES * full : width], edge_ref[k, at, : LANES - rest]], axis=1
+                )
+            value = pltpu.roll(value, lax.rem(target + 8 - lax.rem(p, 8), 8), 0)
+            return jnp.concatenate([value] * (rows // 8), axis=0)
+
         for t in range(tiles):
             inc_x = jnp.where(lane == 0, east_right(t - 1), east_right(t)) - east(t)
             here = q(t)
-            halo = tile_of(halo_ref, p, t)
-            low0, low1, high0, high1 = (halo[k : k + 1] for k in range(4))
             cn = tile_of(cn_ref, level, t)
             chn = chn_s[level, :, LANES * t : LANES * (t + 1)]
-            cs = tile_of(cs_ref, level, t)
-            q_north = jnp.where(row == rows - 1, high0, pltpu.roll(here, rows - 1, 0))
+            q_north = jnp.where(row == rows - 1, edge(1, t, 7), pltpu.roll(here, rows - 1, 0))
             dy = q_north - here
-            dy_low = here[0:1] - low1
-            sy = min_mod(dy, jnp.where(row == 0, dy_low, pltpu.roll(dy, 1, 0)))
-            sy_high = min_mod(high1 - high0, dy[rows - 1 : rows])
-            sy_north = jnp.where(row == rows - 1, sy_high, pltpu.roll(sy, rows - 1, 0))
+            dy_south = jnp.where(row == 0, here - edge(3, t, 0), pltpu.roll(dy, 1, 0))
+            sy = min_mod(dy, dy_south)
+            sy_north = jnp.where(row == rows - 1, edge(2, t, 7), pltpu.roll(sy, rows - 1, 0))
             north = upwind(cn, chn, here, sy, q_north, sy_north)
-            sy_low = min_mod(dy_low, low1 - low0)
-            south_row = upwind(cs, second(cs), low1, sy_low, here[0:1], sy[0:1])
-            south = jnp.where(row == 0, south_row, pltpu.roll(north, 1, 0))
+            south = jnp.where(row == 0, edge(0, t, 0), pltpu.roll(north, 1, 0))
             put(t, here, inc_x + (rs * south - rn * north))
+
+    def respond():
+        half = width // 2
+        filters = spectrum_ref.shape[0]
+        spot = lax.broadcasted_iota(jnp.int32, (rows, filters), 0)
+        picked = jnp.zeros((rows, filters), jnp.int32)
+        for j in range(rows):
+            picked = jnp.where(spot == j, index_ref[device * rows + j], picked)
+        one_hot = picked == lax.broadcasted_iota(jnp.int32, (rows, filters), 1)
+        one_hot = one_hot.astype(jnp.float32).astype(jnp.bfloat16)
+        for start in range(0, width, 2 * CHUNK):
+            span = slice(start, min(start + 2 * CHUNK, width))
+            value = spectrum_ref[:, span]
+            chosen = jnp.zeros((rows, span.stop - start), jnp.float32)
+            for _ in range(3):
+                piece = value.astype(jnp.bfloat16)
+                chosen = chosen + jnp.dot(one_hot, piece, preferred_element_type=jnp.float32)
+                value = value - piece.astype(jnp.float32)
+            chosen_s[:, span] = chosen
+        blocks = 4 * deep // CHUNK
+        chosen_s[:, width:] = jnp.zeros((rows, CHUNK * blocks - width), jnp.float32)
+        column = lax.broadcasted_iota(jnp.int32, (rows, CHUNK), 1)
+        parts = []
+        for b in range(blocks):
+            here = column + CHUNK * b
+            weight = jnp.where((here == 0) | (here == half), 1.0 / width, 2.0 / width)
+            value = chosen_s[:, CHUNK * b : CHUNK * (b + 1)] * weight
+            for _ in range(3):
+                piece = value.astype(jnp.bfloat16)
+                parts.append(piece)
+                value = value - piece.astype(jnp.float32)
+        moved = jnp.dot(jnp.concatenate(parts, axis=0), order_ref[...], preferred_element_type=jnp.float32)
+        moved = moved.reshape(blocks, 3, rows, CHUNK)
+        moved = moved[:, 0] + moved[:, 1] + moved[:, 2]
+        low_half = lane < LANES // 2
+        for b in range(blocks):
+            at = 2 * deep + LANES * b
+            resp_ref[:, at : at + LANES] = moved[b, :, LANES:]
+        for b in range(0, blocks, 2):
+            at = LANES // 2 * b
+            a, c = moved[b, :, :LANES], moved[b + 1, :, :LANES]
+            resp_ref[:, at : at + LANES] = jnp.where(low_half, a, pltpu.roll(c, LANES // 2, 1))
+            resp_ref[:, deep + at : deep + at + LANES] = jnp.where(
+                low_half, pltpu.roll(a, LANES // 2, 1), c
+            )
 
     @pl.when(jnp.logical_not(polar))
     def _():
@@ -185,7 +371,9 @@
                 size = LANES if t < full else rest
                 out_ref[p, :, LANES * t : LANES * t + size] = (here + inc)[:, :size]
 
+            q_copy(p).wait()
             increments(p, lax.rem(p, levels), put)
+            out_copy(p).start()
             return carry
 
         lax.fori_loop(0, planes, plane, 0)
@@ -198,6 +386,7 @@
                     inc = jnp.where(lane < rest, inc, 0.0)
                 inc_s[:, LANES * t : LANES * (t + 1)] = inc
 
+            q_copy(p).wait()
             increments(p, lax.rem(p, levels), put)
             x0, x1, x2, x3 = (inc_s[:, part * k : part * k + deep] for k in range(4))
             a, b = x0 + x2, x1 + x3
@@ -208,6 +397,7 @@
 
         lax.fori_loop(0, planes, plane, 0)
         total = planes * rows
+        respond()
 
         def forward(y, matrix, at):
             coefficients = jnp.dot(y, matrix, preferred_element_type=jnp.float32)
@@ -247,11 +437,9 @@
                     q_ref[:, :, start : start + size]
                     + value.reshape(planes, rows, CHUNK)[:, :, :size]
                 )
-
-
-def shifted(x, axis, by):
-    count = lax.axis_size(axis)
-    return lax.ppermute(x, axis, [(i, i + by) for i in range(count) if 0 <= i + by < count])
+        over_planes(lambda p: out_copy(p).start())
+
+    over_planes(lambda p: out_copy(p).wait())
 
 
 def on_device(tracers, east_courant, north_courant, spectrum, filter_index):
@@ -262,50 +450,41 @@
     part = width // 4
     deep = up_to(part, CHUNK)
     wide = up_to(width, LANES)
+    stacked = up_to(planes + levels, 8)
     q = tracers.reshape(planes, rows, width)
     kind = jnp.bfloat16
-    up = jnp.concatenate(
-        [
-            q[:, rows - 2 :].astype(kind).reshape(2 * planes, width),
-            north_courant[:, rows - 1].astype(kind),
-        ],
-        axis=0,
-    )
-    low = shifted(up, "lon", 1)
-    high = shifted(q[:, :2].astype(kind).reshape(2 * planes, width), "lon", -1)
-    halo = jnp.concatenate(
-        [low[: 2 * planes].reshape(planes, 2, width), high.reshape(planes, 2, width)], axis=1
-    ).astype(jnp.float32)
-    south_courant = low[2 * planes :].astype(jnp.float32).reshape(levels, 1, width)
-    spacing = math.pi / (rows * devices)
-    where = (device * rows + jnp.arange(rows, dtype=jnp.int32)).astype(jnp.float32)
-    center = jnp.sin((where + 0.5) * spacing)
-    ratio = jnp.stack([jnp.sin((where + 1.0) * spacing) / center, jnp.sin(where * spacing) / center])
-    ratio = jnp.broadcast_to(ratio[:, :, None], (2, rows, LANES))
-    quarter = devices // 4
-    polar = ((device < quarter) | (device >= devices - quarter)).astype(jnp.int32).reshape(1)
-    half = width // 2
-    chosen = jnp.take(spectrum, lax.dynamic_slice_in_dim(filter_index, device * rows, rows), axis=0)
-    column = np.arange(width)
-    weight = np.where((column == 0) | (column == half), 1.0 / width, 2.0 / width).astype(np.float32)
-    chosen = chosen * weight[None, :]
-    zeros = jnp.zeros((rows, deep - part), jnp.float32)
-    response = jnp.concatenate(
-        [
-            chosen[:, 0 : half + 1 : 4], chosen[:, half + 4 :: 4], zeros,
-            chosen[:, 2 : half + 1 : 4], chosen[:, half + 2 :: 4], zeros,
-            chosen[:, 1 : half + 1 : 2], chosen[:, half + 1 :: 2], zeros, zeros,
-        ],
-        axis=1,
-    )
-    matrices = [jnp.asarray(m) for m in make_matrices(width)]
     vmem = pl.BlockSpec(memory_space=pltpu.VMEM)
-    out = pl.pallas_call(
-        functools.partial(kernel, width),
-        out_shape=jax.ShapeDtypeStruct(q.shape, jnp.float32),
-        in_specs=[pl.BlockSpec(memory_space=pltpu.SMEM)] + [vmem] * 7 + [pl.BlockSpec(memory_space=pl.ANY)] * 4,
+    smem = pl.BlockSpec(memory_space=pltpu.SMEM)
+    anywhere = pl.BlockSpec(memory_space=pl.ANY)
+    edge = pl.pallas_call(
+        functools.partial(exchange, devices),
+        out_shape=jax.ShapeDtypeStruct((4, stacked, width), jnp.float32),
+        in_specs=[anywhere] * 2,
         out_specs=vmem,
         scratch_shapes=[
+            pltpu.VMEM((planes, 8, width), jnp.float32),
+            pltpu.VMEM((planes, 8, width), jnp.float32),
+            pltpu.VMEM((levels, 8, width), jnp.float32),
+            pltpu.VMEM((2, 2 * stacked, width), jnp.float32),
+        ]
+        + [pltpu.VMEM((2 * stacked, width), kind)] * 4
+        + [pltpu.SemaphoreType.DMA((3,)), pltpu.SemaphoreType.DMA((2,)), pltpu.SemaphoreType.DMA((2,))],
+        compiler_params=pltpu.CompilerParams(
+            collective_id=0, has_side_effects=True, vmem_limit_bytes=56 * 2**20
+        ),
+    )(q, north_courant)
+    matrices = [jnp.asarray(m) for m in make_matrices(width)]
+    out = pl.pallas_call(
+        functools.partial(kernel, width, devices),
+        out_shape=jax.ShapeDtypeStruct(q.shape, jnp.float32),
+        in_specs=[smem, smem, anywhere] + [vmem] * 5 + [anywhere] * 4,
+        out_specs=anywhere,
+        scratch_shapes=[
+            pltpu.VMEM((planes, rows, width), jnp.float32),
+            pltpu.VMEM((planes, rows, width), jnp.float32),
+            pltpu.VMEM((rows, 4 * deep), jnp.float32),
+            pltpu.VMEM((rows, 4 * deep), jnp.float32),
+            pltpu.VMEM((2, rows, LANES), jnp.float32),
             pltpu.VMEM((levels, rows, wide), jnp.float32),
             pltpu.VMEM((levels, rows, wide), jnp.float32),
             pltpu.VMEM((rows, 3 * part + deep + LANES), jnp.float32),
@@ -313,9 +492,12 @@
             pltpu.VMEM((planes * rows, 4 * deep), kind),
         ]
         + [pltpu.VMEM(m.shape, kind) for m in matrices]
-        + [pltpu.SemaphoreType.DMA((4,))],
+        + [pltpu.SemaphoreType.DMA((n,)) for n in (4, planes, planes)],
         compiler_params=pltpu.CompilerParams(vmem_limit_bytes=56 * 2**20),
-    )(polar, q, east_courant, north_courant, south_courant, halo, ratio, response, *matrices)
+    )(
+        device.astype(jnp.int32).reshape(1), filter_index, q, east_courant, north_courant, edge,
+        spectrum, jnp.asarray(make_order()), *matrices,
+    )
     return out.reshape(tracers.shape)
 
 

time: 44.8 us -> 33.8 us (0.75)
  the two profiles are of different devices: /device:TPU:1 before, /device:TPU:27 now
where the time goes in v2:
time: 33.8 us; the launch traced here: 33.7 us
  Pallas kernels  33.7 us (100%)
    pallas_call x1, Pallas kernels, on_device(): pl.pallas_call(functools.partial(kernel, width, devices), out_shape=jax.S...  22.5 us
    pallas_call x1, Pallas kernels, on_device(): pl.pallas_call(functools.partial(exchange, devices), out_shape=jax.ShapeD...  11.2 us

profile of v2, /device:TPU:27, one launch (start us, length us, event | category | flops | bytes accessed | tf_op | source)
XLA Modules:
  0.0 33.7 jit_solution(60504605500697900)
XLA Ops:
  0.0 11.2 %shard_map.100.edge_ref = f32[4,24,2880]{2,1,0:T(8,128)} custom-call(f32[20,16,2880]{2,1,0:T(8,128)} %bitcast.3, f32[4,16,2880]{2,1,0:T(8,128)} %cn_ref.1), custom_call_target="tpu_custom_call" | custom-call | tf_op jit(solution)/shard_map/pallas_call | solution.py:459
  11.3 22.5 %shard_map.101 = f32[20,16,2880]{2,1,0:T(8,128)} custom-call(s32[1]{0:T(128)} %bitcast.where_ref, s32[256]{0:T(256)} %index_ref.1, f32[20,16,2880]{2,1,0:T(8,128)} %bitcast.4, f32[4,16,2880]{2,1,0:T(8,128)} %ce_ref.1, f32[4,16,2880]{2,1,0:T(8,128)} %cn_ref.1, f32[4,24,2880]{2,1,0:T(8,128)} %shard_map.100.edge_ref, f32[64,2880]{1,0:T(8,128)} %spectrum_ref.1, ...), custom_call_target="tpu_custom_call" | custom-call | tf_op jit(solution)/shard_map/pallas_call | solution.py:477

commit v3 on v2

--- a/solution.py
+++ b/solution.py
@@ -56,8 +56,79 @@
     return order.astype(ml_dtypes.bfloat16)
 
 
-def exchange(count, q_hbm, cn_hbm, edge_ref, south_s, north_s, cn_s, packs, up_s, down_s, low_s, high_s,
-             local, send, recv):
+def tile_of(ref, at, t):
+    width = ref.shape[-1]
+    if LANES * (t + 1) <= width:
+        return ref[at, :, LANES * t : LANES * (t + 1)]
+    start = LANES * t
+    return jnp.concatenate([ref[at, :, start:width], ref[at, :, : start + LANES - width]], axis=1)
+
+
+def east_west(width, rows, load_q, load_c, load_ch, put):
+    tiles = -(-width // LANES)
+    rest = width % LANES
+    lane = lax.broadcasted_iota(jnp.int32, (rows, LANES), 1)
+    memo = {}
+
+    def cached(function):
+        def call(t):
+            key = (function.__name__, t)
+            if key not in memo:
+                memo[key] = function(t)
+            return memo[key]
+
+        return call
+
+    def wrapped(load, t):
+        if t >= 0:
+            return load(min(t, tiles - 1))
+        return pltpu.roll(load(tiles - 1), LANES - rest, 1) if rest else load(tiles - 1)
+
+    @cached
+    def q(t):
+        return wrapped(load_q, t)
+
+    @cached
+    def q_left(t):
+        return pltpu.roll(q(t), LANES - 1, 1)
+
+    @cached
+    def q_east(t):
+        return jnp.where(lane == LANES - 1, q_left(min(t + 1, tiles - 1)), q_left(t))
+
+    @cached
+    def d(t):
+        return q_east(t) - q(t)
+
+    @cached
+    def d_right(t):
+        return pltpu.roll(d(t), 1, 1)
+
+    @cached
+    def s(t):
+        return min_mod(d(t), jnp.where(lane == 0, d_right(max(t - 1, -1)), d_right(t)))
+
+    @cached
+    def s_left(t):
+        return pltpu.roll(s(t), LANES - 1, 1)
+
+    @cached
+    def east(t):
+        s_east = jnp.where(lane == LANES - 1, s_left(min(t + 1, tiles - 1)), s_left(t))
+        c = wrapped(load_c, t)
+        ch = wrapped(load_ch, t)
+        return upwind(c, ch, q(t), s(t), q_east(t), s_east)
+
+    @cached
+    def east_right(t):
+        return pltpu.roll(east(t), 1, 1)
+
+    for t in range(tiles):
+        put(t, jnp.where(lane == 0, east_right(t - 1), east_right(t)) - east(t))
+
+
+def exchange(count, q_hbm, ce_hbm, cn_hbm, edge_ref, x_hbm, south_s, north_s, cn_s, ce_s, che_s, x_s, packs, up_s, down_s, low_s, high_s,
+             local, send, recv, x_sems):
     planes, rows, width = q_hbm.shape
     levels = cn_hbm.shape[0]
     deep = edge_ref.shape[1]
@@ -67,6 +138,7 @@
         pltpu.make_async_copy(q_hbm.at[:, pl.ds(rows - 8, 8), :], north_s, local.at[0]),
         pltpu.make_async_copy(cn_hbm.at[:, pl.ds(rows - 8, 8), :], cn_s, local.at[1]),
         pltpu.make_async_copy(q_hbm.at[:, pl.ds(0, 8), :], south_s, local.at[2]),
+        pltpu.make_async_copy(ce_hbm, ce_s, local.at[3]),
     ]
     for load in loads:
         load.start()
@@ -125,6 +197,41 @@
     @pl.when(me > 0)
     def _():
         down.start()
+
+    loads[3].wait()
+    tiles = -(-width // LANES)
+
+    def prepare(level, carry):
+        for t in range(tiles):
+            che_s[level, :, LANES * t : LANES * (t + 1)] = second(tile_of(ce_s, level, t))
+        return carry
+
+    lax.fori_loop(0, levels, prepare, 0)
+
+    def x_copy(p):
+        return pltpu.make_async_copy(x_s.at[p], x_hbm.at[p], x_sems.at[p])
+
+    def plane(p, carry):
+        level = lax.rem(p, levels)
+
+        def put(t, value):
+            size = min(LANES, width - LANES * t)
+            x_s[p, :, LANES * t : LANES * t + size] = value[:, :size]
+
+        def load_q(t):
+            return jnp.concatenate([tile_of(south_s, p, t), tile_of(north_s, p, t)], axis=0)
+
+        east_west(
+            width, rows, load_q, lambda t: tile_of(ce_s, level, t),
+            lambda t: che_s[level, :, LANES * t : LANES * (t + 1)], put,
+        )
+        x_copy(p).start()
+        return carry
+
+    lax.fori_loop(0, planes, plane, 0)
+
+    @pl.when(me > 0)
+    def _():
         up.wait_recv()
 
     @pl.when(me == 0)
@@ -162,6 +269,12 @@
     def _():
         down.wait_send()
 
+    def finish(p, carry):
+        x_copy(p).wait()
+        return carry
+
+    lax.fori_loop(0, planes, finish, 0)
+
 
 def min_mod(a, b):
     return jnp.maximum(jnp.minimum(a, jnp.maximum(b, 0.0)), jnp.minimum(b, 0.0))
@@ -176,12 +289,12 @@
     return c * (jnp.where(c > 0.0, 0.5, -0.5) - 0.5 * c)
 
 
-def kernel(width, count, where_ref, index_ref, q_hbm, ce_ref, cn_ref, edge_ref, spectrum_ref, order_ref,
+def kernel(width, count, where_ref, index_ref, q_hbm, x_hbm, cn_ref, edge_ref, spectrum_ref, order_ref,
            even_hbm, odd_hbm, even_t_hbm, odd_t_hbm, out_hbm,
-           q_ref, out_ref, chosen_s, resp_ref, ratio_s, che_s, chn_s, inc_s, y_s, s_s,
-           even_s, odd_s, even_t_s, odd_t_s, sems, in_sems, out_sems):
+           q_ref, x_ref, out_ref, chosen_s, resp_ref, ratio_s, chn_s, inc_s, y_s, s_s,
+           even_s, odd_s, even_t_s, odd_t_s, sems, in_sems, x_sems, out_sems):
     planes, rows, _ = q_ref.shape
-    levels = ce_ref.shape[0]
+    levels = cn_ref.shape[0]
     part = width // 4
     deep = up_to(part, CHUNK)
     full = width // LANES
@@ -202,6 +315,9 @@
     def q_copy(p):
         return pltpu.make_async_copy(q_hbm.at[p], q_ref.at[p], in_sems.at[p])
 
+    def x_copy(p):
+        return pltpu.make_async_copy(x_hbm.at[p], x_ref.at[p], x_sems.at[p])
+
     def out_copy(p):
         return pltpu.make_async_copy(out_ref.at[p], out_hbm.at[p], out_sems.at[p])
 
@@ -209,6 +325,7 @@
         lax.fori_loop(0, planes, lambda p, carry: (act(p), carry)[1], 0)
 
     over_planes(lambda p: q_copy(p).start())
+    over_planes(lambda p: x_copy(p).start())
 
     @pl.when(polar)
     def _():
@@ -221,77 +338,14 @@
     ratio_s[0] = jnp.sin((place + 1.0) * spacing) / center
     ratio_s[1] = jnp.sin(place * spacing) / center
 
-    def tile_of(ref, at, t):
-        if t < full:
-            return ref[at, :, LANES * t : LANES * (t + 1)]
-        return jnp.concatenate(
-            [ref[at, :, LANES * full : width], ref[at, :, : LANES - rest]], axis=1
-        )
-
     def prepare(level, carry):
         for t in range(tiles):
-            che_s[level, :, LANES * t : LANES * (t + 1)] = second(tile_of(ce_ref, level, t))
             chn_s[level, :, LANES * t : LANES * (t + 1)] = second(tile_of(cn_ref, level, t))
         return carry
 
     lax.fori_loop(0, levels, prepare, 0)
 
     def increments(p, level, put):
-        memo = {}
-
-        def cached(function):
-            def call(t):
-                key = (function.__name__, t)
-                if key not in memo:
-                    memo[key] = function(t)
-                return memo[key]
-
-            return call
-
-        def wrapped(load, t):
-            if t >= 0:
-                return load(min(t, tiles - 1))
-            return pltpu.roll(load(tiles - 1), LANES - rest, 1) if rest else load(tiles - 1)
-
-        @cached
-        def q(t):
-            return wrapped(lambda k: tile_of(q_ref, p, k), t)
-
-        @cached
-        def q_left(t):
-            return pltpu.roll(q(t), LANES - 1, 1)
-
-        @cached
-        def q_east(t):
-            return jnp.where(lane == LANES - 1, q_left(min(t + 1, tiles - 1)), q_left(t))
-
-        @cached
-        def d(t):
-            return q_east(t) - q(t)
-
-        @cached
-        def d_right(t):
-            return pltpu.roll(d(t), 1, 1)
-
-        @cached
-        def s(t):
-            return min_mod(d(t), jnp.where(lane == 0, d_right(max(t - 1, -1)), d_right(t)))
-
-        @cached
-        def s_left(t):
-            return pltpu.roll(s(t), LANES - 1, 1)
-
-        @cached
-        def east(t):
-            s_east = jnp.where(lane == LANES - 1, s_left(min(t + 1, tiles - 1)), s_left(t))
-            c = wrapped(lambda k: tile_of(ce_ref, level, k), t)
-            ch = wrapped(lambda k: che_s[level, :, LANES * k : LANES * (k + 1)], t)
-            return upwind(c, ch, q(t), s(t), q_east(t), s_east)
-
-        @cached
-        def east_right(t):
-            return pltpu.roll(east(t), 1, 1)
-
         rn, rs = ratio_s[0], ratio_s[1]
 
         def edge(k, t, target):
@@ -306,8 +360,8 @@
             return jnp.concatenate([value] * (rows // 8), axis=0)
 
         for t in range(tiles):
-            inc_x = jnp.where(lane == 0, east_right(t - 1), east_right(t)) - east(t)
-            here = q(t)
+            inc_x = tile_of(x_ref, p, t)
+            here = tile_of(q_ref, p, t)
             cn = tile_of(cn_ref, level, t)
             chn = chn_s[level, :, LANES * t : LANES * (t + 1)]
             q_north = jnp.where(row == rows - 1, edge(1, t, 7), pltpu.roll(here, rows - 1, 0))
@@ -372,6 +426,7 @@
                 out_ref[p, :, LANES * t : LANES * t + size] = (here + inc)[:, :size]
 
             q_copy(p).wait()
+            x_copy(p).wait()
             increments(p, lax.rem(p, levels), put)
             out_copy(p).start()
             return carry
@@ -387,6 +442,7 @@
                 inc_s[:, LANES * t : LANES * (t + 1)] = inc
 
             q_copy(p).wait()
+            x_copy(p).wait()
             increments(p, lax.rem(p, levels), put)
             x0, x1, x2, x3 = (inc_s[:, part * k : part * k + deep] for k in range(4))
             a, b = x0 + x2, x1 + x3
@@ -456,46 +512,52 @@
     vmem = pl.BlockSpec(memory_space=pltpu.VMEM)
     smem = pl.BlockSpec(memory_space=pltpu.SMEM)
     anywhere = pl.BlockSpec(memory_space=pl.ANY)
-    edge = pl.pallas_call(
+    edge, along = pl.pallas_call(
         functools.partial(exchange, devices),
-        out_shape=jax.ShapeDtypeStruct((4, stacked, width), jnp.float32),
-        in_specs=[anywhere] * 2,
-        out_specs=vmem,
+        out_shape=(
+            jax.ShapeDtypeStruct((4, stacked, width), jnp.float32),
+            jax.ShapeDtypeStruct(q.shape, jnp.float32),
+        ),
+        in_specs=[anywhere] * 3,
+        out_specs=(vmem, anywhere),
         scratch_shapes=[
             pltpu.VMEM((planes, 8, width), jnp.float32),
             pltpu.VMEM((planes, 8, width), jnp.float32),
             pltpu.VMEM((levels, 8, width), jnp.float32),
+            pltpu.VMEM((levels, rows, width), jnp.float32),
+            pltpu.VMEM((levels, rows, wide), jnp.float32),
+            pltpu.VMEM((planes, rows, width), jnp.float32),
             pltpu.VMEM((2, 2 * stacked, width), jnp.float32),
         ]
         + [pltpu.VMEM((2 * stacked, width), kind)] * 4
-        + [pltpu.SemaphoreType.DMA((3,)), pltpu.SemaphoreType.DMA((2,)), pltpu.SemaphoreType.DMA((2,))],
+        + [pltpu.SemaphoreType.DMA((n,)) for n in (4, 2, 2, planes)],
         compiler_params=pltpu.CompilerParams(
             collective_id=0, has_side_effects=True, vmem_limit_bytes=56 * 2**20
         ),
-    )(q, north_courant)
+    )(q, east_courant, north_courant)
     matrices = [jnp.asarray(m) for m in make_matrices(width)]
     out = pl.pallas_call(
         functools.partial(kernel, width, devices),
         out_shape=jax.ShapeDtypeStruct(q.shape, jnp.float32),
-        in_specs=[smem, smem, anywhere] + [vmem] * 5 + [anywhere] * 4,
+        in_specs=[smem, smem, anywhere] + [anywhere] + [vmem] * 4 + [anywhere] * 4,
         out_specs=anywhere,
         scratch_shapes=[
+            pltpu.VMEM((planes, rows, width), jnp.float32),
             pltpu.VMEM((planes, rows, width), jnp.float32),
             pltpu.VMEM((planes, rows, width), jnp.float32),
             pltpu.VMEM((rows, 4 * deep), jnp.float32),
             pltpu.VMEM((rows, 4 * deep), jnp.float32),
             pltpu.VMEM((2, rows, LANES), jnp.float32),
             pltpu.VMEM((levels, rows, wide), jnp.float32),
-            pltpu.VMEM((levels, rows, wide), jnp.float32),
             pltpu.VMEM((rows, 3 * part + deep + LANES), jnp.float32),
             pltpu.VMEM((planes * rows, 4 * deep), kind),
             pltpu.VMEM((planes * rows, 4 * deep), kind),
         ]
         + [pltpu.VMEM(m.shape, kind) for m in matrices]
-        + [pltpu.SemaphoreType.DMA((n,)) for n in (4, planes, planes)],
+        + [pltpu.SemaphoreType.DMA((n,)) for n in (4, planes, planes, planes)],
         compiler_params=pltpu.CompilerParams(vmem_limit_bytes=56 * 2**20),
     )(
-        device.astype(jnp.int32).reshape(1), filter_index, q, east_courant, north_courant, edge,
+        device.astype(jnp.int32).reshape(1), filter_index, q, along, north_courant, edge,
         spectrum, jnp.asarray(make_order()), *matrices,
     )
     return out.reshape(tracers.shape)

time: 33.8 us -> 31.3 us (0.926)
  the two profiles are of different devices: /device:TPU:27 before, /device:TPU:1 now
where the time goes in v3:
time: 31.3 us; the launch traced here: 31.2 us
  Pallas kernels  31.2 us (100%)
    pallas_call x1, Pallas kernels, on_device(): pl.pallas_call(functools.partial(kernel, width, devices), out_shape=jax.S...  17.6 us
    pallas_call x1, Pallas kernels, on_device(): pl.pallas_call(functools.partial(exchange, devices), out_shape=(jax.Shape...  13.6 us

profile of v3, /device:TPU:1, one launch (start us, length us, event | category | flops | bytes accessed | tf_op | source)
XLA Modules:
  0.0 31.2 jit_solution(17214015223833342594)
XLA Ops:
  0.0 13.6 %shard_map.100 = (f32[4,24,2880]{2,1,0:T(8,128)}, f32[20,16,2880]{2,1,0:T(8,128)}) custom-call(f32[20,16,2880]{2,1,0:T(8,128)} %bitcast.3, f32[4,16,2880]{2,1,0:T(8,128)} %ce_hbm.1, f32[4,16,2880]{2,1,0:T(8,128)} %cn_ref.1), custom_call_target="tpu_custom_call" | custom-call | tf_op jit(solution)/shard_map/pallas_call | solution.py:515
  13.6 17.6 %shard_map.101 = f32[20,16,2880]{2,1,0:T(8,128)} custom-call(s32[1]{0:T(128)} %bitcast.where_ref, s32[256]{0:T(256)} %index_ref.1, f32[20,16,2880]{2,1,0:T(8,128)} %bitcast.4, f32[20,16,2880]{2,1,0:T(8,128)} %get-tuple-element.7.x_hbm, f32[4,16,2880]{2,1,0:T(8,128)} %cn_ref.1, f32[4,24,2880]{2,1,0:T(8,128)} %get-tuple-element.8.edge_ref, ...), custom_call_target="tpu_custom_call" | custom-call | tf_op jit(solution)/shard_map/pallas_call | solution.py:539

commit v4 on v3

--- a/solution.py
+++ b/solution.py
@@ -211,9 +211,7 @@
     def x_copy(p):
         return pltpu.make_async_copy(x_s.at[p], x_hbm.at[p], x_sems.at[p])
 
-    def plane(p, carry):
-        level = lax.rem(p, levels)
-
+    def plane(p, level):
         def put(t, value):
             size = min(LANES, width - LANES * t)
             x_s[p, :, LANES * t : LANES * t + size] = value[:, :size]
@@ -225,10 +223,16 @@
             width, rows, load_q, lambda t: tile_of(ce_s, level, t),
             lambda t: che_s[level, :, LANES * t : LANES * (t + 1)], put,
         )
-        x_copy(p).start()
+
+    def together(level, carry):
+        group = [field * levels + level for field in range(planes // levels)]
+        for p in group:
+            plane(p, level)
+        for p in group:
+            x_copy(p).start()
         return carry
 
-    lax.fori_loop(0, planes, plane, 0)
+    lax.fori_loop(0, levels, together, 0)
 
     @pl.when(me > 0)
     def _():
@@ -324,8 +328,13 @@
     def over_planes(act):
         lax.fori_loop(0, planes, lambda p, carry: (act(p), carry)[1], 0)
 
-    over_planes(lambda p: q_copy(p).start())
-    over_planes(lambda p: x_copy(p).start())
+    def begin(level, carry):
+        for field in range(planes // levels):
+            q_copy(field * levels + level).start()
+            x_copy(field * levels + level).start()
+        return carry
+
+    lax.fori_loop(0, levels, begin, 0)
 
     @pl.when(polar)
     def _():
@@ -420,38 +429,51 @@
 
     @pl.when(jnp.logical_not(polar))
     def _():
-        def plane(p, carry):
+        def plane(p, level):
             def put(t, here, inc):
                 size = LANES if t < full else rest
                 out_ref[p, :, LANES * t : LANES * t + size] = (here + inc)[:, :size]
 
-            q_copy(p).wait()
-            x_copy(p).wait()
-            increments(p, lax.rem(p, levels), put)
-            out_copy(p).start()
+            increments(p, level, put)
+
+        def together(level, carry):
+            group = [field * levels + level for field in range(planes // levels)]
+            for p in group:
+                q_copy(p).wait()
+                x_copy(p).wait()
+            for p in group:
+                plane(p, level)
+            for p in group:
+                out_copy(p).start()
             return carry
 
-        lax.fori_loop(0, planes, plane, 0)
+        lax.fori_loop(0, levels, together, 0)
 
     @pl.when(polar)
     def _():
-        def plane(p, carry):
+        def plane(p, level, slot):
             def put(t, here, inc):
                 if t >= full:
                     inc = jnp.where(lane < rest, inc, 0.0)
-                inc_s[:, LANES * t : LANES * (t + 1)] = inc
-
-            q_copy(p).wait()
-            x_copy(p).wait()
-            increments(p, lax.rem(p, levels), put)
-            x0, x1, x2, x3 = (inc_s[:, part * k : part * k + deep] for k in range(4))
+                inc_s[slot, :, LANES * t : LANES * (t + 1)] = inc
+
+            increments(p, level, put)
+            x0, x1, x2, x3 = (inc_s[slot, :, part * k : part * k + deep] for k in range(4))
             a, b = x0 + x2, x1 + x3
             where = pl.ds(pl.multiple_of(p * rows, rows), rows)
             for k, y in enumerate((a + b, a - b, x0 - x2, x1 - x3)):
                 y_s[where, deep * k : deep * (k + 1)] = y.astype(jnp.bfloat16)
+
+        def together(level, carry):
+            group = [field * levels + level for field in range(planes // levels)]
+            for p in group:
+                q_copy(p).wait()
+                x_copy(p).wait()
+            for slot, p in enumerate(group):
+                plane(p, level, slot)
             return carry
 
-        lax.fori_loop(0, planes, plane, 0)
+        lax.fori_loop(0, levels, together, 0)
         total = planes * rows
         respond()
 
@@ -549,7 +571,7 @@
             pltpu.VMEM((rows, 4 * deep), jnp.float32),
             pltpu.VMEM((2, rows, LANES), jnp.float32),
             pltpu.VMEM((levels, rows, wide), jnp.float32),
-            pltpu.VMEM((rows, 3 * part + deep + LANES), jnp.float32),
+            pltpu.VMEM((fields, rows, 3 * part + deep + LANES), jnp.float32),
             pltpu.VMEM((planes * rows, 4 * deep), kind),
             pltpu.VMEM((planes * rows, 4 * deep), kind),
         ]

time: 31.3 us -> 92.5 us (2.96)
  Pallas kernels: 31.2 us -> 92.4 us
    pallas_call x1, Pallas kernels: 13.6 us -> 76.5 us  [on_device(): pl.pallas_call(functools.partial(exchange, devices), out_shape=(jax.Shape...]
    pallas_call x1, Pallas kernels: 17.6 us -> 15.9 us  [on_device(): pl.pallas_call(functools.partial(kernel, width, devices), out_shape=jax.S...]
where the time goes in v4:
time: 92.5 us; the launch traced here: 92.4 us
  Pallas kernels  92.4 us (100%)
    pallas_call x1, Pallas kernels, on_device(): pl.pallas_call(functools.partial(exchange, devices), out_shape=(jax.Shape...  76.5 us
    pallas_call x1, Pallas kernels, on_device(): pl.pallas_call(functools.partial(kernel, width, devices), out_shape=jax.S...  15.9 us

profile of v4, /device:TPU:1, one launch (start us, length us, event | category | flops | bytes accessed | tf_op | source)
XLA Modules:
  0.0 92.4 jit_solution(11225360926609509196)
XLA Ops:
  0.0 76.5 %shard_map.100 = (f32[4,24,2880]{2,1,0:T(8,128)}, f32[20,16,2880]{2,1,0:T(8,128)}) custom-call(f32[20,16,2880]{2,1,0:T(8,128)} %bitcast.3, f32[4,16,2880]{2,1,0:T(8,128)} %ce_hbm.1, f32[4,16,2880]{2,1,0:T(8,128)} %cn_ref.1), custom_call_target="tpu_custom_call" | custom-call | tf_op jit(solution)/shard_map/pallas_call | solution.py:537
  76.5 15.9 %shard_map.101 = f32[20,16,2880]{2,1,0:T(8,128)} custom-call(s32[1]{0:T(128)} %bitcast.where_ref, s32[256]{0:T(256)} %index_ref.1, f32[20,16,2880]{2,1,0:T(8,128)} %bitcast.4, f32[20,16,2880]{2,1,0:T(8,128)} %get-tuple-element.7.x_hbm, f32[4,16,2880]{2,1,0:T(8,128)} %cn_ref.1, f32[4,24,2880]{2,1,0:T(8,128)} %get-tuple-element.8.edge_ref, ...), custom_call_target="tpu_custom_call" | custom-call | tf_op jit(solution)/shard_map/pallas_call | solution.py:561
